TPU v7x, 512 devices: a whole 4x4x16 slice. The times are simulated.
512 devices in a mesh: section: 16 (over y, z_hi), dp: 32 (over z_lo, x, core).
Axes of the slice: x: 4, y: 4, z: 16 (z_hi: 4, z_lo: 4; z = z_hi * 4 + z_lo), core: 2. Of those that a mesh axis runs over, the one named last changes fastest.
Arguments:
- slab_store: bfloat16 [16, 32, 10, 16, 8192], P('section', 'dp'), may hold values from -600 to 600
- slab_place: int32 [16, 32, 8], P('section', 'dp'), may hold values from 0 to 19, as said below
- cotangent: bfloat16 [16, 32, 128, 8192], P('section', 'dp'), may hold values from -18 to 18
- norm_gain: bfloat16 [16, 8192], P('section'), may hold values from 0.099609375 to 1.8984375
Outputs:
- gain_grad: float32 [16, 8192], P('section')
- inner_prods: float32 [16, 32, 128], P('section', 'dp')
Inputs may be any that keep to these rules, and one draw needn't show every extreme that they name: `slab_place`: A device's 8 entries are distinct. An entry v below 10 names slot v of the device's own store; an entry v of 10 or more names slot v - 10 of the store of the device with the same dp index on section 15 - s. No slot is named twice by the two devices of a mirrored pair. At most 4 entries of a device name the mirrored store, and some device has exactly 4.
All inputs are finite; a program needn't handle non-finite values.
Results may differ from a plain program's by a relative error of at most 0.0003.
Values may be sent and summed in bfloat16 or wider, within the bound.
No kernel may reach another device: no remote copies, remote signals or barrier semaphores. Data moves between devices by JAX's collectives and lax.ppermute only.
A program may use at most 64 MiB of HBM per device.

v0:
```python
import math

import jax
import jax.numpy as jnp
from jax import lax
from jax.sharding import PartitionSpec as P

epsilon = 1e-05


def partner(array, axis, stride):
    return lax.ppermute(array, axis, [(i, i ^ 1 << stride) for i in range(lax.axis_size(axis))])


def shards(slab_store, slab_place, cotangent, norm_gain):
    own_store = slab_store[0, 0]
    places = slab_place[0, 0]
    levels = lax.axis_size("section").bit_length() - 1
    bit_order = list(range(levels))
    remote = own_store
    for bit_index in bit_order:
        remote = partner(remote, "section", bit_index)
    combined = jnp.concatenate([own_store, remote], axis=0)
    fetched_slabs = jnp.take(combined, places, axis=0)
    width = fetched_slabs.shape[-1]
    tok_rows = fetched_slabs.reshape(-1, width).astype(jnp.float32)
    inv_rms = lax.rsqrt(jnp.mean(tok_rows * tok_rows, axis=-1, keepdims=True) + epsilon)
    normed = tok_rows * inv_rms
    cotangents = cotangent[0, 0].astype(jnp.float32)
    partial_grad = jnp.sum(cotangents * normed, axis=0)
    total = lax.psum(partial_grad, "dp")
    gain_grad = total / math.sqrt(lax.axis_size("dp") * tok_rows.shape[0])
    gain_row = norm_gain[0].astype(jnp.float32)
    inner_prods = jnp.sum(normed * gain_row * cotangents, axis=-1) / math.sqrt(width)
    return (gain_grad[None, :], inner_prods[None, None, :])


def solution(mesh):
    placed = (
        P("section", "dp", None, None, None),
        P("section", "dp", None),
        P("section", "dp", None, None),
        P("section", None),
    )
    return jax.shard_map(
        shards,
        mesh=mesh,
        in_specs=placed,
        out_specs=(P("section", None), P("section", "dp", None)),
        check_vma=False,
    )
```

profile of v0, /device:TPU:1, one launch (start us, length us, event | category | flops | bytes accessed | tf_op | source)
XLA Modules:
  0.0 793.7 jit_solution(15558338255335745387)
XLA Ops:
  0.6 9.6 %collective-permute-start = (bf16[10,16,8192]{2,1,0:T(8,128)(2,1)}, bf16[10,16,8192]{2,1,0:T(8,128)(2,1)S(1)}, u32[]{:S(2)}, u32[]{:S(2)}) collective-permute-start(bf16[10,16,8192]{2,1,0:T(8,128)(2,1)} %bitcast.23), channel_id=1, source_target_pairs={{0,32},{32,0},{64,96},{96,64},{128,160},{160,128},{192,224},{224,1... | collective-permute-start | bytes 7864328 | tf_op jit(solution)/shard_map/ppermute | solution.py:12
  10.3 281.2 %collective-permute-done = bf16[10,16,8192]{2,1,0:T(8,128)(2,1)S(1)} collective-permute-done((bf16[10,16,8192]{2,1,0:T(8,128)(2,1)}, bf16[10,16,8192]{2,1,0:T(8,128)(2,1)S(1)}, u32[]{:S(2)}, u32[]{:S(2)}) %collective-permute-start) | collective-permute-done | bytes 2621472 | tf_op jit(solution)/shard_map/ppermute | solution.py:12
  291.5 127.7 %collective-permute-start.1 = (bf16[10,16,8192]{2,1,0:T(8,128)(2,1)S(1)}, bf16[10,16,8192]{2,1,0:T(8,128)(2,1)S(1)}, u32[]{:S(2)}, u32[]{:S(2)}) collective-permute-start(bf16[10,16,8192]{2,1,0:T(8,128)(2,1)S(1)} %collective-permute-done), channel_id=1, source_target_pairs={{0,64},{32,96},{64,0},{96,32},{128,192},{160,224},{192,128},{224,1... | collective-permute-start | bytes 7864328 | tf_op jit(solution)/shard_map/ppermute | solution.py:12
  419.3 112.6 %collective-permute-done.1 = bf16[10,16,8192]{2,1,0:T(8,128)(2,1)S(1)} collective-permute-done((bf16[10,16,8192]{2,1,0:T(8,128)(2,1)S(1)}, bf16[10,16,8192]{2,1,0:T(8,128)(2,1)S(1)}, u32[]{:S(2)}, u32[]{:S(2)}) %collective-permute-start.1) | collective-permute-done | bytes 2621472 | tf_op jit(solution)/shard_map/ppermute | solution.py:12
  531.8 3.2 collective-permute-start.2
  535.0 55.4 %collective-permute-done.2 = bf16[10,16,8192]{2,1,0:T(8,128)(2,1)} collective-permute-done((bf16[10,16,8192]{2,1,0:T(8,128)(2,1)S(1)}, bf16[10,16,8192]{2,1,0:T(8,128)(2,1)}, u32[]{:S(2)}, u32[]{:S(2)}) %collective-permute-start.2) | collective-permute-done | bytes 2621472 | tf_op jit(solution)/shard_map/ppermute | solution.py:12
  590.4 4.8 collective-permute-start.3
  595.2 0.7 compare_and_fusion
  595.9 0.1 broadcast_in_dim.28
  596.0 0.1 broadcast_in_dim.29
  596.1 0.8 mul.59
  596.9 0.7 fusion.3
  597.5 52.1 %collective-permute-done.3 = bf16[10,16,8192]{2,1,0:T(8,128)(2,1)S(1)} collective-permute-done((bf16[10,16,8192]{2,1,0:T(8,128)(2,1)}, bf16[10,16,8192]{2,1,0:T(8,128)(2,1)S(1)}, u32[]{:S(2)}, u32[]{:S(2)}) %collective-permute-start.3) | collective-permute-done | bytes 2621472 | tf_op jit(solution)/shard_map/ppermute | solution.py:12
  649.7 4.5 pad_maximum_fusion
  654.2 3.2 gather_fusion
  657.3 0.7 multiply_reduce_fusion
  658.1 0.1 rsqrt.14
  658.1 0.0 copy-start
  658.1 2.7 fusion.1
  660.8 0.0 copy-done
  660.9 1.2 fusion.2
  662.0 0.5 multiply_bitcast_fusion
  662.6 130.5 %psum.7 = f32[8192]{0:T(1024)S(1)} all-reduce(f32[8192]{0:T(1024)S(1)} %fusion.1), channel_id=1, replica_groups=mesh['section'=16,'dp'=32] {'dp'}, use_global_device_ids=true, to_apply=%region_2.3 | all-reduce | flops 8192 | bytes 65536 | tf_op jit(solution)/shard_map/psum | solution.py:31
  793.1 0.6 broadcast_multiply_fusion
  (2 shorter events, 0.0 us)
Async XLA Ops:
  0.6 290.9 %collective-permute-start = (bf16[10,16,8192]{2,1,0:T(8,128)(2,1)}, bf16[10,16,8192]{2,1,0:T(8,128)(2,1)S(1)}, u32[]{:S(2)}, u32[]{:S(2)}) collective-permute-start(bf16[10,16,8192]{2,1,0:T(8,128)(2,1)} %bitcast.23), channel_id=1, source_target_pairs={{0,32},{32,0},{64,96},{96,64},{128,160},{160,128},{192,224},{224,1... | collective-permute-start | bytes 7864328 | tf_op jit(solution)/shard_map/ppermute | solution.py:12
  291.5 240.3 %collective-permute-start.1 = (bf16[10,16,8192]{2,1,0:T(8,128)(2,1)S(1)}, bf16[10,16,8192]{2,1,0:T(8,128)(2,1)S(1)}, u32[]{:S(2)}, u32[]{:S(2)}) collective-permute-start(bf16[10,16,8192]{2,1,0:T(8,128)(2,1)S(1)} %collective-permute-done), channel_id=1, source_target_pairs={{0,64},{32,96},{64,0},{96,32},{128,192},{160,224},{192,128},{224,1... | collective-permute-start | bytes 7864328 | tf_op jit(solution)/shard_map/ppermute | solution.py:12
  531.8 58.6 %collective-permute-start.2 = (bf16[10,16,8192]{2,1,0:T(8,128)(2,1)S(1)}, bf16[10,16,8192]{2,1,0:T(8,128)(2,1)}, u32[]{:S(2)}, u32[]{:S(2)}) collective-permute-start(bf16[10,16,8192]{2,1,0:T(8,128)(2,1)S(1)} %collective-permute-done.1), channel_id=1, source_target_pairs={{0,128},{32,160},{64,192},{96,224},{128,0},{160,32},{192,64},{224,... | collective-permute-start | bytes 7864328 | tf_op jit(solution)/shard_map/ppermute | solution.py:12
  590.4 59.3 %collective-permute-start.3 = (bf16[10,16,8192]{2,1,0:T(8,128)(2,1)}, bf16[10,16,8192]{2,1,0:T(8,128)(2,1)S(1)}, u32[]{:S(2)}, u32[]{:S(2)}) collective-permute-start(bf16[10,16,8192]{2,1,0:T(8,128)(2,1)} %collective-permute-done.2), channel_id=1, source_target_pairs={{0,256},{32,288},{64,320},{96,352},{128,384},{160,416},{192,448},{... | collective-permute-start | bytes 7864328 | tf_op jit(solution)/shard_map/ppermute | solution.py:12
  658.1 2.7 copy-start
where the time goes:
time: 799 us; the launch traced here: 794 us
  waiting for transfers between devices  501 us (63%)
  starting transfers between devices  145 us (18%)
  blocking collectives  131 us (16%)
  other arithmetic  12.4 us (2%)
    ppermute x4, waiting for transfers between devices, partner(): lax.ppermute(array, axis, [(i, i ^ 1 << stride) for i in range(lax.axis_s...  501 us
    ppermute x4, starting transfers between devices, partner(): lax.ppermute(array, axis, [(i, i ^ 1 << stride) for i in range(lax.axis_s...  145 us
    psum x1, blocking collectives, shards(): total = lax.psum(partial_grad, 'dp')  131 us
  transfers between devices with their start and end apart: 4, of which 4 were waited for; matrix products, arithmetic and copies ran while one was open for 0% of the time, Pallas kernels for 0%

commit v1 on v0

v1 whole, which is shorter than its diff:
```python
import functools
import math

import jax
import jax.numpy as jnp
from jax import lax
from jax.experimental import pallas as pl
from jax.experimental.pallas import tpu as pltpu
from jax.sharding import PartitionSpec as P

epsilon = 1e-05
MOST = 4
LANES = 128
STEP = 512
SMEM = pl.BlockSpec(memory_space=pltpu.SMEM)
VMEM = pl.BlockSpec(memory_space=pltpu.VMEM)
HBM = pl.BlockSpec(memory_space=pl.ANY)
LIMIT = pltpu.CompilerParams(vmem_limit_bytes=24 * 1024 * 1024)


def mirror(array):
    size = lax.axis_size("section")
    return lax.ppermute(array, "section", [(i, size - 1 - i) for i in range(size)])


def nth_away(places, slots, n):
    seen = position = slot = found = jnp.int32(0)
    for k in range(places.shape[0]):
        place = places[k]
        away = (place >= slots).astype(jnp.int32)
        hit = away * (seen == n).astype(jnp.int32)
        position = position + hit * k
        slot = slot + hit * (place - slots)
        found = found + hit
        seen = seen + away
    return position, slot, found


def count_away(places, slots):
    return sum((places[k] >= slots).astype(jnp.int32) for k in range(places.shape[0]))


def fold(block):
    total = block[:, :LANES]
    for j in range(LANES, block.shape[1], LANES):
        total = total + block[:, j : j + LANES]
    return total


def slab_terms(x, c, g, grad):
    width = x.shape[1]
    squares = jnp.zeros((x.shape[0], LANES), jnp.float32)
    for j in range(0, width, STEP):
        rows = x[:, j : j + STEP].astype(jnp.float32)
        squares = squares + fold(rows * rows)
    inv_rms = lax.rsqrt(jnp.sum(squares, axis=1, keepdims=True) / width + epsilon)
    inner = jnp.zeros((x.shape[0], LANES), jnp.float32)
    for j in range(0, width, STEP):
        product = x[:, j : j + STEP].astype(jnp.float32) * inv_rms * c[:, j : j + STEP].astype(jnp.float32)
        grad[:, j : j + STEP] += product[:8] + product[8:]
        inner = inner + fold(product * g[:, j : j + STEP].astype(jnp.float32))
    return inner


def pack_kernel(groups, slots, places, far_places, array, most, *refs):
    outs, sems = refs[:-1], refs[-1]
    copies = []
    for out, numbers in zip(outs, groups):
        for i, n in enumerate(numbers):
            _, slot, _ = nth_away(far_places, slots, n)
            copies.append(pltpu.make_async_copy(array.at[slot], out.at[i], sems.at[len(copies)]))
            copies[-1].start()
    most[0] = jnp.maximum(count_away(places, slots), count_away(far_places, slots))
    for copy in copies:
        copy.wait()


def pack(places, far_places, store, groups):
    shapes = [jax.ShapeDtypeStruct((len(numbers),) + store.shape[1:], store.dtype) for numbers in groups]
    return pl.pallas_call(
        functools.partial(pack_kernel, groups, store.shape[0]),
        out_shape=[jax.ShapeDtypeStruct((1,), jnp.int32)] + shapes,
        in_specs=[SMEM, SMEM, HBM],
        out_specs=[SMEM] + [VMEM] * len(groups),
        scratch_shapes=[pltpu.SemaphoreType.DMA((sum(map(len, groups)),))],
        compiler_params=LIMIT,
    )(places, far_places, store)


def own_kernel(slots, places, x, c, g, grad, inner):
    step = pl.program_id(0)

    @pl.when(step == 0)
    def _():
        grad[...] = jnp.zeros_like(grad)

    here = places[step] < slots

    @pl.when(here)
    def _():
        inner[0] = slab_terms(x.at[0], c.at[0], g, grad)

    @pl.when(jnp.logical_not(here))
    def _():
        inner[...] = jnp.zeros_like(inner)


def own_terms(places, store, cotangents, gain):
    slots, slab, width = store.shape
    count = places.shape[0]
    return pl.pallas_call(
        functools.partial(own_kernel, slots),
        out_shape=(
            jax.ShapeDtypeStruct((8, width), jnp.float32),
            jax.ShapeDtypeStruct((count + 1, slab, LANES), jnp.float32),
        ),
        grid_spec=pltpu.PrefetchScalarGridSpec(
            num_scalar_prefetch=1,
            grid=(count,),
            in_specs=[
                pl.BlockSpec((1, slab, width), lambda i, places: (jnp.where(places[i] < slots, places[i], 0), 0, 0)),
                pl.BlockSpec((1, slab, width), lambda i, places: (i, 0, 0)),
                pl.BlockSpec((1, width), lambda i, places: (0, 0)),
            ],
            out_specs=[
                pl.BlockSpec((8, width), lambda i, places: (0, 0)),
                pl.BlockSpec((1, slab, LANES), lambda i, places: (i, 0, 0)),
            ],
        ),
        compiler_params=LIMIT,
    )(places, store, cotangents, gain)


def far_kernel(slots, first, places, x, c, g, grad_in, inner_in, grad, inner):
    step = pl.program_id(0)

    @pl.when(step == 0)
    def _():
        grad[...] = grad_in[...]

    @pl.when(nth_away(places, slots, step + first)[2] > 0)
    def _():
        inner[0] = slab_terms(x.at[0], c.at[0], g, grad)


def far_terms(places, slots, first, x, cotangents, gain, grad, inner):
    number, slab, width = x.shape
    spare = inner.shape[0] - 1

    def line(i, places):
        position, _, found = nth_away(places, slots, i + first)
        return jnp.where(found > 0, position, spare), 0, 0

    whole = pl.BlockSpec((8, width), lambda i, places: (0, 0))
    return pl.pallas_call(
        functools.partial(far_kernel, slots, first),
        out_shape=(jax.ShapeDtypeStruct(grad.shape, grad.dtype), jax.ShapeDtypeStruct(inner.shape, inner.dtype)),
        grid_spec=pltpu.PrefetchScalarGridSpec(
            num_scalar_prefetch=1,
            grid=(number,),
            in_specs=[
                pl.BlockSpec((1, slab, width), lambda i, places: (i, 0, 0)),
                pl.BlockSpec((1, slab, width), lambda i, places: (nth_away(places, slots, i + first)[0], 0, 0)),
                pl.BlockSpec((1, width), lambda i, places: (0, 0)),
                whole,
                HBM,
            ],
            out_specs=[whole, pl.BlockSpec((1, slab, LANES), line)],
        ),
        input_output_aliases={5: 1},
        compiler_params=LIMIT,
    )(places, x, cotangents, gain, grad, inner)


def sum_over_dp(row):
    size = lax.axis_size("dp")
    shares = lax.all_to_all(row.reshape(size, -1), "dp", 0, 0)
    share = jnp.sum(shares, axis=0)
    whole = lax.all_to_all(jnp.broadcast_to(share[None], (size,) + share.shape), "dp", 0, 0)
    return whole.reshape(-1)


def shards(slab_store, slab_place, cotangent, norm_gain):
    store = slab_store[0, 0]
    places = slab_place[0, 0]
    slots, slab, width = store.shape
    count = places.shape[0]
    cotangents = cotangent[0, 0].reshape(count, slab, width)

    far_places = mirror(places)
    most, *packs = pack(places, far_places, store, [range(n) for n in range(1, MOST + 1)])

    def exchange(number):
        def branch(packs, cotangents):
            grad, inner = own_terms(places, store, cotangents, norm_gain)
            if number:
                received = mirror(packs[number - 1])
                grad, inner = far_terms(places, slots, 0, received, cotangents, norm_gain, grad, inner)
            return grad, inner

        return branch

    grad, inner = lax.switch(most[0], [exchange(number) for number in range(MOST + 1)], packs, cotangents)

    tokens = lax.axis_size("dp") * count * slab
    gain_grad = sum_over_dp(jnp.sum(grad, axis=0)) / math.sqrt(tokens)
    inner_prods = jnp.sum(inner[:count], axis=-1).reshape(-1) / math.sqrt(width)
    return gain_grad[None, :], inner_prods[None, None, :]


def solution(mesh):
    placed = (
        P("section", "dp", None, None, None),
        P("section", "dp", None),
        P("section", "dp", None, None),
        P("section", None),
    )
    return jax.shard_map(
        shards,
        mesh=mesh,
        in_specs=placed,
        out_specs=(P("section", None), P("section", "dp", None)),
        check_vma=False,
    )
```

time: 799 us -> 137 us (0.17)
  waiting for transfers between devices: 501 us -> 80.9 us
  blocking collectives: 131 us -> 12.8 us
  starting transfers between devices: 145 us -> 29.1 us
  other arithmetic: 12.4 us -> 1.36 us
  Pallas kernels: 0 us -> 10.7 us
    ppermute x4 -> x2, waiting for transfers between devices: 501 us -> 73.7 us  [mirror(): lax.ppermute(array, 'section', [(i, size - 1 - i) for i in range(size)])]
    psum x1 -> x0, blocking collectives: 131 us -> none  [shards(): total = lax.psum(partial_grad, 'dp')]
    ppermute x4 -> x2, starting transfers between devices: 145 us -> 25.2 us  [mirror(): lax.ppermute(array, 'section', [(i, size - 1 - i) for i in range(size)])]
    all_to_all x0 -> x1, blocking collectives: none -> 12.8 us  [sum_over_dp(): shares = lax.all_to_all(row.reshape(size, -1), 'dp', 0, 0)]
    pallas_call x0 -> x3, Pallas kernels: none -> 10.7 us  [the longest x1 5.22 us: own_terms(): pl.pallas_call(functools.partial(own_kernel, slots), out_shape=(jax.Shape...]
  transfers between devices with their start and end apart: 4 -> 3, of which waited for: 4 -> 3; matrix products, arithmetic and copies ran while one was open for 0% -> 0% of each run, Pallas kernels for 0% -> 4%
where the time goes in v1:
time: 137 us
  waiting for transfers between devices  80.9 us (59%)
  starting transfers between devices  29.1 us (21%)
  blocking collectives  12.8 us (9%)
  Pallas kernels  10.7 us (8%)
    ppermute x2, waiting for transfers between devices, mirror(): lax.ppermute(array, 'section', [(i, size - 1 - i) for i in range(size)])  73.7 us
    ppermute x2, starting transfers between devices, mirror(): lax.ppermute(array, 'section', [(i, size - 1 - i) for i in range(size)])  25.2 us
    all_to_all x1, blocking collectives, sum_over_dp(): shares = lax.all_to_all(row.reshape(size, -1), 'dp', 0, 0)  12.8 us
    all_to_all x1, waiting for transfers between devices, sum_over_dp(): lax.all_to_all(jnp.broadcast_to(share[None], (size,) + share.shape), 'dp'...  7.23 us
    pallas_call x1, Pallas kernels, own_terms(): pl.pallas_call(functools.partial(own_kernel, slots), out_shape=(jax.Shape...  5.22 us
    all_to_all x1, starting transfers between devices, sum_over_dp(): lax.all_to_all(jnp.broadcast_to(share[None], (size,) + share.shape), 'dp'...  3.9 us
    pallas_call x1, Pallas kernels, pack(): pl.pallas_call(functools.partial(pack_kernel, groups, store.shape[0]), ou...  3.68 us
  transfers between devices with their start and end apart: 3, of which 3 were waited for; matrix products, arithmetic and copies ran while one was open for 0% of the time, Pallas kernels for 4%

profile of v1, /device:TPU:1, one launch (start us, length us, event | category | flops | bytes accessed | tf_op | source)
XLA Modules:
  0.0 137.1 jit_solution(10995453615931026719)
XLA Ops:
  0.6 0.0 copy-start.2
  0.6 0.0 copy-start.1
  0.7 0.0 copy-start
  0.7 15.9 %collective-permute-start.4 = (s32[8]{0:T(128)}, s32[8]{0:T(128)S(1)}, u32[]{:S(2)}, u32[]{:S(2)}) collective-permute-start(s32[8]{0:T(128)} %bitcast.18), channel_id=1, source_target_pairs={{0,480},{32,448},{64,416},{96,384},{128,352},{160,320},{192,288},{... | collective-permute-start | bytes 104 | tf_op jit(solution)/shard_map/ppermute | solution.py:23
  16.5 1.0 collective-permute-done.4.far_places
  17.6 3.7 %shard_map.59 = (s32[1]{0:T(128)}, bf16[1,16,8192]{2,1,0:T(8,128)(2,1)S(1)}, bf16[2,16,8192]{2,1,0:T(8,128)(2,1)}, bf16[3,16,8192]{2,1,0:T(8,128)(2,1)}, bf16[4,16,8192]{2,1,0:T(8,128)(2,1)S(1)}) custom-call(s32[8]{0:T(128)} %bitcast.19, s32[8]{0:T(128)S(1)} %collective-permute-done.4.far_places, bf16[10,16,8192]{2,1,0:T(8,128)(2,1)} %bitcast.11), custom_call_target="tpu_custom_call" | custom-call | tf_op jit(solution)/shard_map/pallas_call | solution.py:80
  21.9 0.0 copy-done.2
  21.9 0.0 copy-done.1
  21.9 0.0 copy-done
  21.9 89.2 %conditional.1 = (f32[8,8192]{1,0:T(8,128)S(1)}, f32[1,1,128]{2,1,0:T(1,128)S(1)}) conditional(s32[]{:T(128)} %bitcast.2, (s32[8]{0:T(128)S(1)}, bf16[10,16,8192]{2,1,0:T(8,128)(2,1)}, bf16[8,16,8192]{2,1,0:T(8,128)(2,1)S(1)}, bf16[1,8192]{1,0:T(2,128)(2,1)S(1)}) %tuple.59, (bf16[1,16,8192]{2,1,0:T(8,128)(2,1)S(1)}, ...), branch_computations={%region_0.2_spmd, %region_2.4_spmd, %region_4.6_spmd, %region_6.8_... | conditional | flops 16256 | bytes 4261432 | solution.py:203
  22.0 9.3 %collective-permute-start.3 = (bf16[4,16,8192]{2,1,0:T(8,128)(2,1)S(1)}, bf16[4,16,8192]{2,1,0:T(8,128)(2,1)S(1)}, u32[]{:S(2)}, u32[]{:S(2)}) collective-permute-start(bf16[4,16,8192]{2,1,0:T(8,128)(2,1)S(1)} %get-tuple-element.93), channel_id=1, source_target_pairs={{0,480},{32,448},{64,416},{96,384},{128,352},{160,320},{192,288},{... | collective-permute-start | bytes 3145736 | tf_op jit(solution)/shard_map/cond/branch_4_fun/ppermute | solution.py:23
  31.3 5.2 %branch_4_fun.2 = (f32[8,8192]{1,0:T(8,128)S(1)}, f32[9,16,128]{2,1,0:T(8,128)S(1)}) custom-call(s32[8]{0:T(128)S(1)} %get-tuple-element.92.places, bf16[10,16,8192]{2,1,0:T(8,128)(2,1)} %get-tuple-element.96.x, bf16[8,16,8192]{2,1,0:T(8,128)(2,1)S(1)} %get-tuple-element.94.c, bf16[1,8192]{1,0:T(2,128)(2,1)S(1)} %get-tuple-element.95.g), custom_call_target="tpu_custom_call" | custom-call | tf_op jit(solution)/shard_map/cond/branch_4_fun/pallas_call | solution.py:111
  36.6 72.6 %collective-permute-done.3.x = bf16[4,16,8192]{2,1,0:T(8,128)(2,1)S(1)} collective-permute-done((bf16[4,16,8192]{2,1,0:T(8,128)(2,1)S(1)}, bf16[4,16,8192]{2,1,0:T(8,128)(2,1)S(1)}, u32[]{:S(2)}, u32[]{:S(2)}) %collective-permute-start.3) | collective-permute-done | bytes 1048608 | tf_op jit(solution)/shard_map/cond/branch_4_fun/ppermute | solution.py:23
  109.2 1.8 %branch_4_fun.3 = (f32[8,8192]{1,0:T(8,128)S(1)}, f32[9,16,128]{2,1,0:T(8,128)S(1)}) custom-call(s32[8]{0:T(128)S(1)} %get-tuple-element.92.places, bf16[4,16,8192]{2,1,0:T(8,128)(2,1)S(1)} %collective-permute-done.3.x, bf16[8,16,8192]{2,1,0:T(8,128)(2,1)S(1)} %get-tuple-element.94.c, ...), custom_call_target="tpu_custom_call", output_to_operand_aliasing={{1}: (5, {})} | custom-call | tf_op jit(solution)/shard_map/cond/branch_4_fun/pallas_call | solution.py:155
  111.0 0.1 slice_reduce_fusion.4
  111.1 0.1 reshape.47
  111.2 0.1 reduce_sum.47
  111.3 12.8 %all_to_all.15 = f32[32,1,256]{2,1,0:T(1,128)S(1)} all-to-all(f32[32,1,256]{2,1,0:T(1,128)S(1)} %bitcast.17), channel_id=1, replica_groups=mesh['section'=16,'dp'=32] {'dp'}, dimensions={0} | all-to-all | bytes 65536 | tf_op jit(solution)/shard_map/all_to_all | solution.py:177
  124.1 0.1 reduce_sum.48
  124.2 0.6 broadcast_in_dim.2
  124.8 3.9 %all-to-all-start.1 = ((f32[32,1,256]{2,1,0:T(1,128)}), f32[32,1,256]{2,1,0:T(1,128)S(1)}, u32[]{:S(2)}, u32[]{:S(2)}) async-start(f32[32,1,256]{2,1,0:T(1,128)} %broadcast_in_dim.2), calls=%async_computation.1 | async-start | bytes 65536 | tf_op jit(solution)/shard_map/all_to_all | solution.py:179
  128.7 0.5 broadcast_multiply_fusion.1
  129.2 7.2 %all-to-all-done.1 = f32[32,1,256]{2,1,0:T(1,128)S(1)} async-done(((f32[32,1,256]{2,1,0:T(1,128)}), f32[32,1,256]{2,1,0:T(1,128)S(1)}, u32[]{:S(2)}, u32[]{:S(2)}) %all-to-all-start.1) | async-done | bytes 32800 | tf_op jit(solution)/shard_map/all_to_all | solution.py:179
  136.4 0.6 broadcast_multiply_fusion
Async XLA Ops:
  0.6 21.3 %copy-start.2 = (s32[1,1,8]{2,1,0:T(1,128)S(1)}, s32[1,1,8]{2,1,0:T(1,128)}, u32[]{:S(2)}) copy-start(s32[1,1,8]{2,1,0:T(1,128)} %param.10) | copy-start | bytes 100
  0.6 21.3 %copy-start.1 = (bf16[1,8192]{1,0:T(2,128)(2,1)S(1)}, bf16[1,8192]{1,0:T(2,128)(2,1)}, u32[]{:S(2)}) copy-start(bf16[1,8192]{1,0:T(2,128)(2,1)} %param.12) | copy-start | bytes 49156
  0.7 21.3 %copy-start = (bf16[1,1,128,8192]{3,2,1,0:T(8,128)(2,1)S(1)}, bf16[1,1,128,8192]{3,2,1,0:T(8,128)(2,1)}, u32[]{:S(2)}) copy-start(bf16[1,1,128,8192]{3,2,1,0:T(8,128)(2,1)} %param.11) | copy-start | bytes 6291460
  0.7 16.9 %collective-permute-start.4 = (s32[8]{0:T(128)}, s32[8]{0:T(128)S(1)}, u32[]{:S(2)}, u32[]{:S(2)}) collective-permute-start(s32[8]{0:T(128)} %bitcast.18), channel_id=1, source_target_pairs={{0,480},{32,448},{64,416},{96,384},{128,352},{160,320},{192,288},{... | collective-permute-start | bytes 104 | tf_op jit(solution)/shard_map/ppermute | solution.py:23
  22.0 87.2 %collective-permute-start.3 = (bf16[4,16,8192]{2,1,0:T(8,128)(2,1)S(1)}, bf16[4,16,8192]{2,1,0:T(8,128)(2,1)S(1)}, u32[]{:S(2)}, u32[]{:S(2)}) collective-permute-start(bf16[4,16,8192]{2,1,0:T(8,128)(2,1)S(1)} %get-tuple-element.93), channel_id=1, source_target_pairs={{0,480},{32,448},{64,416},{96,384},{128,352},{160,320},{192,288},{... | collective-permute-start | bytes 3145736 | tf_op jit(solution)/shard_map/cond/branch_4_fun/ppermute | solution.py:23
  124.8 11.7 %all-to-all-start.1 = ((f32[32,1,256]{2,1,0:T(1,128)}), f32[32,1,256]{2,1,0:T(1,128)S(1)}, u32[]{:S(2)}, u32[]{:S(2)}) async-start(f32[32,1,256]{2,1,0:T(1,128)} %broadcast_in_dim.2), calls=%async_computation.1 | async-start | bytes 65536 | tf_op jit(solution)/shard_map/all_to_all | solution.py:179

commit v2 on v1

v2 whole, which is shorter than its diff:
```python
import functools
import math

import jax
import jax.numpy as jnp
from jax import lax
from jax.experimental import pallas as pl
from jax.experimental.pallas import tpu as pltpu
from jax.sharding import PartitionSpec as P

epsilon = 1e-05
MOST = 4
LANES = 128
STEP = 512
SMEM = pl.BlockSpec(memory_space=pltpu.SMEM)
VMEM = pl.BlockSpec(memory_space=pltpu.VMEM)
HBM = pl.BlockSpec(memory_space=pl.ANY)
LIMIT = pltpu.CompilerParams(vmem_limit_bytes=24 * 1024 * 1024)


def mirror(array):
    size = lax.axis_size("section")
    return lax.ppermute(array, "section", [(i, size - 1 - i) for i in range(size)])


def nth_away(places, slots, n):
    seen = position = slot = found = jnp.int32(0)
    for k in range(places.shape[0]):
        place = places[k]
        away = (place >= slots).astype(jnp.int32)
        hit = away * (seen == n).astype(jnp.int32)
        position = position + hit * k
        slot = slot + hit * (place - slots)
        found = found + hit
        seen = seen + away
    return position, slot, found


def count_away(places, slots):
    return sum((places[k] >= slots).astype(jnp.int32) for k in range(places.shape[0]))


def fold(block):
    total = block[:, :LANES]
    for j in range(LANES, block.shape[1], LANES):
        total = total + block[:, j : j + LANES]
    return total


def slab_terms(x, c, g, grad):
    width = grad.shape[1]
    steps = [slice(j, j + STEP) for j in range(0, width, STEP)]
    squares = sum(fold(jnp.square(x(step))) for step in steps)
    inv_rms = lax.rsqrt(jnp.sum(squares, axis=1, keepdims=True) / width + epsilon)
    inner = jnp.zeros_like(squares)
    for step in steps:
        product = x(step) * inv_rms * c(step)
        grad[:, step] += product[:8] + product[8:] if product.shape[0] == 16 else product
        inner = inner + fold(product * g[:, step].astype(jnp.float32))
    return inner


def columns(ref, rows=slice(None)):
    return lambda step: ref[:, step].astype(jnp.float32)[rows]


def choose_kernel(slots, places, far_places, store, cotangents, branch, whole, half, sem):
    mine, theirs = count_away(places, slots), count_away(far_places, slots)
    more = jnp.abs(mine - theirs)
    branch[0] = 3 * jnp.minimum(mine, theirs) + more

    @pl.when(mine > theirs)
    def _():
        pltpu.make_async_copy(cotangents.at[nth_away(places, slots, mine - 1)[0]], whole, sem).start()

    @pl.when(mine <= theirs)
    def _():
        slot = nth_away(far_places, slots, theirs - jnp.maximum(more, 1))[1]
        pltpu.make_async_copy(store.at[slot], whole, sem).start()

    pltpu.make_async_copy(store.at[0], whole, sem).wait()
    for j in range(0, whole.shape[1], STEP):
        rows = whole[:, j : j + STEP].astype(jnp.float32)
        half[:, j : j + STEP] = jnp.where(mine > theirs, rows[8:], rows[:8]).astype(half.dtype)


def choose(places, far_places, store, cotangents):
    slab = jax.ShapeDtypeStruct(store.shape[1:], store.dtype)
    half = jax.ShapeDtypeStruct((8, store.shape[2]), store.dtype)
    return pl.pallas_call(
        functools.partial(choose_kernel, store.shape[0]),
        out_shape=[jax.ShapeDtypeStruct((1,), jnp.int32), slab, half],
        in_specs=[SMEM, SMEM, HBM, HBM],
        out_specs=[SMEM, VMEM, VMEM],
        scratch_shapes=[pltpu.SemaphoreType.DMA],
        compiler_params=LIMIT,
    )(places, far_places, store, cotangents)


def pack_kernel(slots, far_places, store, out, sems):
    copies = []
    for n in range(out.shape[0]):
        slot = nth_away(far_places, slots, n)[1]
        copies.append(pltpu.make_async_copy(store.at[slot], out.at[n], sems.at[n]))
        copies[-1].start()
    for copy in copies:
        copy.wait()


def pack(far_places, store, number):
    return pl.pallas_call(
        functools.partial(pack_kernel, store.shape[0]),
        out_shape=jax.ShapeDtypeStruct((number,) + store.shape[1:], store.dtype),
        in_specs=[SMEM, HBM],
        out_specs=VMEM,
        scratch_shapes=[pltpu.SemaphoreType.DMA((number,))],
        compiler_params=LIMIT,
    )(far_places, store)


def even_kernel(slots, more, places, far_places, y, x, c, g, far_g, grad_in, inner_in, grad, inner, back, back_grad):
    mine, theirs = count_away(places, slots), count_away(far_places, slots)
    width = grad.shape[1]
    grad[...] = grad_in[...]
    back[...] = jnp.zeros_like(back)
    given = columns(y)

    @pl.when(mine > theirs)
    def _():
        rows = slice(0, y.shape[0])
        inner[...] = jnp.zeros_like(inner)
        inner[0, rows] = slab_terms(given, columns(c.at[0], rows), g, grad)

    @pl.when(mine < theirs)
    def _():
        rows = slice(x.shape[1] - y.shape[0], None)
        back_grad[...] = jnp.zeros_like(back_grad)
        sums = jnp.sum(slab_terms(columns(x.at[0], rows), given, far_g, back_grad), axis=1, keepdims=True)
        token = lax.broadcasted_iota(jnp.int32, (y.shape[0], LANES), 0) + rows.start
        lane = lax.broadcasted_iota(jnp.int32, (y.shape[0], LANES), 1)
        back[:, width:] = jnp.sum(jnp.where(token == lane, sums, 0.0), axis=0, keepdims=True)
        for j in range(0, width, STEP):
            back[:, j : j + STEP] = jnp.sum(back_grad[:, j : j + STEP], axis=0, keepdims=True)


def even_terms(places, far_places, more, y, store, cotangents, gain, far_gain, grad, inner):
    slots, slab, width = store.shape
    spare = inner.shape[0] - 1

    def own_item(places, far_places):
        mine, theirs = count_away(places, slots), count_away(far_places, slots)
        return nth_away(places, slots, mine - more)[0], mine > theirs

    def far_item(i, places, far_places):
        return nth_away(far_places, slots, count_away(far_places, slots) - 1)[1], 0, 0

    def line(i, places, far_places):
        position, ours = own_item(places, far_places)
        return jnp.where(ours, position, spare), 0, 0

    def whole(*shape):
        return pl.BlockSpec(shape, lambda i, places, far_places: (0,) * len(shape))

    return pl.pallas_call(
        functools.partial(even_kernel, slots, more),
        out_shape=(
            jax.ShapeDtypeStruct(grad.shape, grad.dtype),
            jax.ShapeDtypeStruct(inner.shape, inner.dtype),
            jax.ShapeDtypeStruct((1, width + LANES), jnp.float32),
        ),
        grid_spec=pltpu.PrefetchScalarGridSpec(
            num_scalar_prefetch=2,
            grid=(1,),
            in_specs=[
                whole(*y.shape),
                pl.BlockSpec((1, slab, width), far_item),
                pl.BlockSpec((1, slab, width), lambda i, places, far_places: (own_item(places, far_places)[0], 0, 0)),
                whole(1, width),
                whole(1, width),
                whole(8, width),
                HBM,
            ],
            out_specs=[whole(8, width), pl.BlockSpec((1, slab, LANES), line), whole(1, width + LANES)],
            scratch_shapes=[pltpu.VMEM((8, width), jnp.float32)],
        ),
        cost_estimate=pl.CostEstimate(flops=4 * 10**10, bytes_accessed=10**6, transcendentals=0),
        input_output_aliases={8: 1},
        compiler_params=LIMIT,
    )(places, far_places, y, store, cotangents, gain, far_gain, grad, inner)


def own_kernel(slots, places, x, c, g, grad, inner):
    step = pl.program_id(0)

    @pl.when(step == 0)
    def _():
        grad[...] = jnp.zeros_like(grad)

    here = places[step] < slots

    @pl.when(here)
    def _():
        inner[0] = slab_terms(columns(x.at[0]), columns(c.at[0]), g, grad)

    @pl.when(jnp.logical_not(here))
    def _():
        inner[...] = jnp.zeros_like(inner)


def own_terms(places, store, cotangents, gain):
    slots, slab, width = store.shape
    count = places.shape[0]
    return pl.pallas_call(
        functools.partial(own_kernel, slots),
        out_shape=(
            jax.ShapeDtypeStruct((8, width), jnp.float32),
            jax.ShapeDtypeStruct((count + 1, slab, LANES), jnp.float32),
        ),
        grid_spec=pltpu.PrefetchScalarGridSpec(
            num_scalar_prefetch=1,
            grid=(count,),
            in_specs=[
                pl.BlockSpec((1, slab, width), lambda i, places: (jnp.where(places[i] < slots, places[i], 0), 0, 0)),
                pl.BlockSpec((1, slab, width), lambda i, places: (i, 0, 0)),
                pl.BlockSpec((1, width), lambda i, places: (0, 0)),
            ],
            out_specs=[
                pl.BlockSpec((8, width), lambda i, places: (0, 0)),
                pl.BlockSpec((1, slab, LANES), lambda i, places: (i, 0, 0)),
            ],
        ),
        compiler_params=LIMIT,
    )(places, store, cotangents, gain)


def write_row(grad, back, row):
    for j in range(0, row.shape[1], STEP):
        row[:, j : j + STEP] = jnp.sum(grad[:, j : j + STEP], axis=0, keepdims=True) + back[:, j : j + STEP]


def far_kernel(slots, places, x, c, g, grad_in, back, inner_in, row, inner, grad):
    step = pl.program_id(0)

    @pl.when(step == 0)
    def _():
        grad[...] = grad_in[...]

    inner[0] = slab_terms(columns(x.at[0]), columns(c.at[0]), g, grad)

    @pl.when(step == pl.num_programs(0) - 1)
    def _():
        write_row(grad, back, row)


def far_terms(places, slots, x, cotangents, gain, grad, back, inner):
    number, slab, width = x.shape

    def item(i, places):
        return nth_away(places, slots, i)[0], 0, 0

    def whole(*shape):
        return pl.BlockSpec(shape, lambda i, places: (0,) * len(shape))

    return pl.pallas_call(
        functools.partial(far_kernel, slots),
        out_shape=(jax.ShapeDtypeStruct((1, width), jnp.float32), jax.ShapeDtypeStruct(inner.shape, inner.dtype)),
        grid_spec=pltpu.PrefetchScalarGridSpec(
            num_scalar_prefetch=1,
            grid=(number,),
            in_specs=[
                pl.BlockSpec((1, slab, width), lambda i, places: (i, 0, 0)),
                pl.BlockSpec((1, slab, width), item),
                whole(1, width),
                whole(8, width),
                whole(1, width + LANES),
                HBM,
            ],
            out_specs=[whole(1, width), pl.BlockSpec((1, slab, LANES), item)],
            scratch_shapes=[pltpu.VMEM((8, width), jnp.float32)],
        ),
        input_output_aliases={6: 1},
        compiler_params=LIMIT,
    )(places, x, cotangents, gain, grad, back, inner)


def gradient_row(grad, back):
    return pl.pallas_call(
        write_row,
        out_shape=jax.ShapeDtypeStruct((1, grad.shape[1]), jnp.float32),
        in_specs=[VMEM, VMEM],
        out_specs=VMEM,
    )(grad, back)


def sum_over_dp(row):
    size = lax.axis_size("dp")
    shares = lax.all_to_all(row.reshape(size, -1), "dp", 0, 0)
    share = jnp.sum(shares, axis=0)
    whole = lax.all_to_all(jnp.broadcast_to(share[None], (size,) + share.shape), "dp", 0, 0)
    return whole.reshape(-1)


def shards(slab_store, slab_place, cotangent, norm_gain):
    store = slab_store[0, 0]
    places = slab_place[0, 0]
    slots, slab, width = store.shape
    count = places.shape[0]
    cotangents = cotangent[0, 0].reshape(count, slab, width)

    far_places = mirror(places)
    branch, whole, half = choose(places, far_places, store, cotangents)

    def exchange(fewer, more):
        def run(whole, half, cotangents):
            back = jnp.zeros((1, width + LANES), jnp.float32)
            if more:
                y = mirror(half if more == 1 else whole)
                far_gain = mirror(norm_gain)
            if fewer:
                received = mirror(pack(far_places, store, fewer))
            grad, inner = own_terms(places, store, cotangents, norm_gain)
            if more:
                grad, inner, back = even_terms(places, far_places, more, y, store, cotangents, norm_gain, far_gain, grad, inner)
                back = mirror(back)
            if fewer:
                row, inner = far_terms(places, slots, received, cotangents, norm_gain, grad, back, inner)
            else:
                row = gradient_row(grad, back)
            return row, inner, back[:, width : width + slab]

        return run

    branches = [exchange(fewer, more if fewer + more <= MOST else 0) for fewer in range(MOST + 1) for more in range(3)]
    row, inner, back = lax.switch(branch[0], branches[: 3 * MOST + 1], whole, half, cotangents)

    tokens = lax.axis_size("dp") * count * slab
    gain_grad = sum_over_dp(row[0]) / math.sqrt(tokens)
    places, row = lax.optimization_barrier((places, row))
    away = (places >= slots).astype(jnp.int32)
    last = (away > 0) & (jnp.cumsum(away) == jnp.sum(away))
    inner_prods = jnp.sum(inner[:count], axis=-1) + jnp.where(last[:, None], back, 0.0)
    inner_prods = inner_prods.reshape(-1) / math.sqrt(width)
    return gain_grad[None, :], inner_prods[None, None, :]


def solution(mesh):
    placed = (
        P("section", "dp", None, None, None),
        P("section", "dp", None),
        P("section", "dp", None, None),
        P("section", None),
    )
    return jax.shard_map(
        shards,
        mesh=mesh,
        in_specs=placed,
        out_specs=(P("section", None), P("section", "dp", None)),
        check_vma=False,
    )
```

time: 137 us -> 135 us (0.985)
  starting transfers between devices: 29.1 us -> 72.4 us
  waiting for transfers between devices: 80.9 us -> 46.8 us
  blocking collectives: 12.8 us -> 0 us
  other arithmetic: 1.36 us -> 3.17 us
    ppermute x2 -> x5, waiting for transfers between devices: 73.7 us -> 33.9 us  [mirror(): lax.ppermute(array, 'section', [(i, size - 1 - i) for i in range(size)])]
    ppermute x2 -> x5, starting transfers between devices: 25.2 us -> 47 us  [mirror(): lax.ppermute(array, 'section', [(i, size - 1 - i) for i in range(size)])]
    all_to_all x0 -> x1, starting transfers between devices: none -> 21.5 us  [sum_over_dp(): shares = lax.all_to_all(row.reshape(size, -1), 'dp', 0, 0)]
    all_to_all x1 -> x0, blocking collectives: 12.8 us -> none  [sum_over_dp(): shares = lax.all_to_all(row.reshape(size, -1), 'dp', 0, 0)]
    all_to_all x0 -> x1, waiting for transfers between devices: none -> 5.86 us  [sum_over_dp(): shares = lax.all_to_all(row.reshape(size, -1), 'dp', 0, 0)]
    reduce_sum x2, other arithmetic: 0.15 us -> 1.56 us  [the longest x1 0.93 us: shards(): jnp.sum(inner[:count], axis=-1) + jnp.where(last[:, None], back, 0.0)]
    pallas_call x2 -> x4, Pallas kernels: 5.48 us -> 5.66 us  [the longest x1 2.19 us: choose(): pl.pallas_call(functools.partial(choose_kernel, store.shape[0]), out_shap...]
  transfers between devices with their start and end apart: 3 -> 7, of which waited for: 3 -> 5; matrix products, arithmetic and copies ran while one was open for 0% -> 2% of each run, Pallas kernels for 4% -> 5%
where the time goes in v2:
time: 135 us
  starting transfers between devices  72.4 us (54%)
  waiting for transfers between devices  46.8 us (35%)
  Pallas kernels  9.81 us (7%)
  other arithmetic  3.17 us (2%)
  between operations  1.38 us (1%)
    ppermute x5, starting transfers between devices, mirror(): lax.ppermute(array, 'section', [(i, size - 1 - i) for i in range(size)])  47 us
    ppermute x5, waiting for transfers between devices, mirror(): lax.ppermute(array, 'section', [(i, size - 1 - i) for i in range(size)])  33.9 us
    all_to_all x1, starting transfers between devices, sum_over_dp(): shares = lax.all_to_all(row.reshape(size, -1), 'dp', 0, 0)  21.5 us
    all_to_all x1, waiting for transfers between devices, sum_over_dp(): lax.all_to_all(jnp.broadcast_to(share[None], (size,) + share.shape), 'dp'...  7.07 us
    all_to_all x1, waiting for transfers between devices, sum_over_dp(): shares = lax.all_to_all(row.reshape(size, -1), 'dp', 0, 0)  5.86 us
    pallas_call x1, Pallas kernels, own_terms(): pl.pallas_call(functools.partial(own_kernel, slots), out_shape=(jax.Shape...  4.15 us
    all_to_all x1, starting transfers between devices, sum_over_dp(): lax.all_to_all(jnp.broadcast_to(share[None], (size,) + share.shape), 'dp'...  3.9 us
  transfers between devices with their start and end apart: 7, of which 5 were waited for; matrix products, arithmetic and copies ran while one was open for 2% of the time, Pallas kernels for 5%

profile of v2, /device:TPU:1, one launch (start us, length us, event | category | flops | bytes accessed | tf_op | source)
XLA Modules:
  0.0 134.9 jit_solution(1227675810175872909)
XLA Ops:
  0.6 0.0 copy-start.17
  0.6 0.0 copy-start.3
  0.7 16.0 %collective-permute-start.31 = (s32[8]{0:T(128)}, s32[8]{0:T(128)S(1)}, u32[]{:S(2)}, u32[]{:S(2)}) collective-permute-start(s32[8]{0:T(128)} %bitcast.39), channel_id=1, source_target_pairs={{0,480},{32,448},{64,416},{96,384},{128,352},{160,320},{192,288},{... | collective-permute-start | bytes 104 | tf_op jit(solution)/shard_map/ppermute | solution.py:23
  16.7 1.0 collective-permute-done.31.far_places
  17.7 2.2 %shard_map.59 = (s32[1]{0:T(128)}, bf16[16,8192]{1,0:T(8,128)(2,1)S(1)}, bf16[8,8192]{1,0:T(8,128)(2,1)S(1)}) custom-call(s32[8]{0:T(128)} %bitcast.40, s32[8]{0:T(128)S(1)} %collective-permute-done.31.far_places, bf16[10,16,8192]{2,1,0:T(8,128)(2,1)} %bitcast.11, bf16[8,16,8192]{2,1,0:T(8,128)(2,1)} %bitcast.25), custom_call_target="tpu_custom_call" | custom-call | tf_op jit(solution)/shard_map/pallas_call | solution.py:90
  20.6 71.6 %conditional.1 = (f32[1,8192]{1,0:T(1,128)}, f32[9,16,128]{2,1,0:T(8,128)}, f32[1,16]{1,0:T(1,128)S(1)}) conditional(s32[]{:T(128)} %bitcast.3, (s32[8]{0:T(128)S(1)}, bf16[10,16,8192]{2,1,0:T(8,128)(2,1)S(1)}, bf16[8,16,8192]{2,1,0:T(8,128)(2,1)}, bf16[1,8192]{1,0:T(2,128)(2,1)S(1)}) %tuple.121, ...), branch_computations={%region_0.0_spmd, %region_1.0_spmd, %region_2.0_spmd, %region_3.0_... | conditional | flops 40000000000 | bytes 13257620 | solution.py:334
  20.6 0.0 copy-start.7
  20.6 9.5 %collective-permute-start.8 = (bf16[8,8192]{1,0:T(8,128)(2,1)S(1)}, bf16[8,8192]{1,0:T(8,128)(2,1)S(1)}, u32[]{:S(2)}, u32[]{:S(2)}) collective-permute-start(bf16[8,8192]{1,0:T(8,128)(2,1)S(1)} %get-tuple-element.184), channel_id=1, source_target_pairs={{0,480},{32,448},{64,416},{96,384},{128,352},{160,320},{192,288},{... | collective-permute-start | bytes 393224 | tf_op jit(solution)/shard_map/cond/branch_4_fun/ppermute | solution.py:23
  30.2 1.9 %collective-permute-start.9 = (bf16[1,8192]{1,0:T(2,128)(2,1)S(1)}, bf16[1,8192]{1,0:T(2,128)(2,1)S(1)}, u32[]{:S(2)}, u32[]{:S(2)}) collective-permute-start(bf16[1,8192]{1,0:T(2,128)(2,1)S(1)} %get-tuple-element.183.g), channel_id=1, source_target_pairs={{0,480},{32,448},{64,416},{96,384},{128,352},{160,320},{192,288},{... | collective-permute-start | bytes 49160 | tf_op jit(solution)/shard_map/cond/branch_4_fun/ppermute | solution.py:23
  32.1 0.6 branch_4_fun.4
  32.7 9.4 %collective-permute-start.7 = (bf16[1,16,8192]{2,1,0:T(8,128)(2,1)S(1)}, bf16[1,16,8192]{2,1,0:T(8,128)(2,1)S(1)}, u32[]{:S(2)}, u32[]{:S(2)}) collective-permute-start(bf16[1,16,8192]{2,1,0:T(8,128)(2,1)S(1)} %branch_4_fun.4), channel_id=1, source_target_pairs={{0,480},{32,448},{64,416},{96,384},{128,352},{160,320},{192,288},{... | collective-permute-start | bytes 786440 | tf_op jit(solution)/shard_map/cond/branch_4_fun/ppermute | solution.py:23
  42.1 4.2 %branch_4_fun.5 = (f32[8,8192]{1,0:T(8,128)S(1)}, f32[9,16,128]{2,1,0:T(8,128)}) custom-call(s32[8]{0:T(128)S(1)} %get-tuple-element.179.places, bf16[10,16,8192]{2,1,0:T(8,128)(2,1)S(1)} %get-tuple-element.181.store.x, bf16[8,16,8192]{2,1,0:T(8,128)(2,1)S(1)} %copy-done.7, bf16[1,8192]{1,0:T(2,128)(2,1)S(1)} %get-tuple-element.183.g), custom_call_target="tpu_custom_call" | custom-call | tf_op jit(solution)/shard_map/cond/branch_4_fun/pallas_call | solution.py:213
  46.3 31.5 %collective-permute-done.9.far_g = bf16[1,8192]{1,0:T(2,128)(2,1)S(1)} collective-permute-done((bf16[1,8192]{1,0:T(2,128)(2,1)S(1)}, bf16[1,8192]{1,0:T(2,128)(2,1)S(1)}, u32[]{:S(2)}, u32[]{:S(2)}) %collective-permute-start.9) | collective-permute-done | bytes 16416 | tf_op jit(solution)/shard_map/cond/branch_4_fun/ppermute | solution.py:23
  77.8 0.0 collective-permute-done.8.y
  77.8 1.4 %branch_4_fun.6 = (f32[8,8192]{1,0:T(8,128)S(1)}, f32[9,16,128]{2,1,0:T(8,128)}, f32[1,8320]{1,0:T(1,128)S(1)}) custom-call(s32[8]{0:T(128)S(1)} %get-tuple-element.179.places, s32[8]{0:T(128)S(1)} %get-tuple-element.180.far_places, bf16[8,8192]{1,0:T(8,128)(2,1)S(1)} %collective-permute-done.8.y, ...), custom_call_target="tpu_custom_call", output_to_operand_aliasing={{1}: (8, {})} | custom-call | flops 40000000000 | bytes 1000000 | tf_op jit(solution)/shard_map/cond/branch_4_fun/pallas_call | solution.py:164
  79.2 10.2 %collective-permute-start.10 = (f32[1,8320]{1,0:T(1,128)S(1)}, f32[1,8320]{1,0:T(1,128)S(1)}, u32[]{:S(2)}, u32[]{:S(2)}) collective-permute-start(f32[1,8320]{1,0:T(1,128)S(1)} %get-tuple-element.188), channel_id=1, source_target_pairs={{0,480},{32,448},{64,416},{96,384},{128,352},{160,320},{192,288},{... | collective-permute-start | bytes 99848 | tf_op jit(solution)/shard_map/cond/branch_4_fun/ppermute | solution.py:23
  89.4 1.3 collective-permute-done.10.back
  90.7 0.0 collective-permute-done.7.x
  90.7 1.5 %branch_4_fun.7 = (f32[1,8192]{1,0:T(1,128)}, f32[9,16,128]{2,1,0:T(8,128)}) custom-call(s32[8]{0:T(128)S(1)} %get-tuple-element.179.places, bf16[1,16,8192]{2,1,0:T(8,128)(2,1)S(1)} %collective-permute-done.7.x, bf16[8,16,8192]{2,1,0:T(8,128)(2,1)S(1)} %copy-done.7, bf16[1,8192]{1,0:T(2,128)(2,1)S(1)} %get-tuple-element.183.g, ...), custom_call_target="tpu_custom_call", output_to_operand_aliasing={{1}: (6, {})} | custom-call | tf_op jit(solution)/shard_map/cond/branch_4_fun/pallas_call | solution.py:264
  92.2 0.6 fusion
  92.8 21.5 %all-to-all-start = ((f32[32,1,256]{2,1,0:T(1,128)}), f32[32,1,256]{2,1,0:T(1,128)S(1)}, u32[]{:S(2)}, u32[]{:S(2)}) async-start(f32[32,1,256]{2,1,0:T(1,128)} %bitcast.4), calls=%async_computation | async-start | bytes 65536 | tf_op jit(solution)/shard_map/all_to_all | solution.py:297
  114.3 0.2 reduce-window.9
  114.5 0.7 bitcast_and_fusion
  115.2 0.9 slice_reduce_fusion
  116.1 5.9 %all-to-all-done = f32[32,1,256]{2,1,0:T(1,128)S(1)} async-done(((f32[32,1,256]{2,1,0:T(1,128)}), f32[32,1,256]{2,1,0:T(1,128)S(1)}, u32[]{:S(2)}, u32[]{:S(2)}) %all-to-all-start) | async-done | bytes 32800 | tf_op jit(solution)/shard_map/all_to_all | solution.py:297
  121.9 0.1 reduce_sum.27
  122.0 0.6 broadcast_in_dim.31
  122.6 3.9 %all-to-all-start.1 = ((f32[32,1,256]{2,1,0:T(1,128)}), f32[32,1,256]{2,1,0:T(1,128)S(1)}, u32[]{:S(2)}, u32[]{:S(2)}) async-start(f32[32,1,256]{2,1,0:T(1,128)} %broadcast_in_dim.31), calls=%async_computation.1 | async-start | bytes 65536 | tf_op jit(solution)/shard_map/all_to_all | solution.py:299
  126.5 0.1 add_multiply_fusion
  126.6 0.6 div.21
  127.2 7.1 %all-to-all-done.1 = f32[32,1,256]{2,1,0:T(1,128)S(1)} async-done(((f32[32,1,256]{2,1,0:T(1,128)}), f32[32,1,256]{2,1,0:T(1,128)S(1)}, u32[]{:S(2)}, u32[]{:S(2)}) %all-to-all-start.1) | async-done | bytes 32800 | tf_op jit(solution)/shard_map/all_to_all | solution.py:299
  134.3 0.6 broadcast_multiply_fusion
  (7 shorter events, 0.0 us)
Async XLA Ops:
  0.6 19.9 %copy-start.17 = (s32[1,1,8]{2,1,0:T(1,128)S(1)}, s32[1,1,8]{2,1,0:T(1,128)}, u32[]{:S(2)}) copy-start(s32[1,1,8]{2,1,0:T(1,128)} %param.18) | copy-start | bytes 100
  0.6 19.9 %copy-start.3 = (bf16[1,1,10,16,8192]{4,3,2,1,0:T(8,128)(2,1)S(1)}, bf16[1,1,10,16,8192]{4,3,2,1,0:T(8,128)(2,1)}, u32[]{:S(2)}) copy-start(bf16[1,1,10,16,8192]{4,3,2,1,0:T(8,128)(2,1)} %param.17) | copy-start | bytes 7864324
  0.7 19.9 %copy-start.16 = (bf16[1,8192]{1,0:T(2,128)(2,1)S(1)}, bf16[1,8192]{1,0:T(2,128)(2,1)}, u32[]{:S(2)}) copy-start(bf16[1,8192]{1,0:T(2,128)(2,1)} %param.20) | copy-start | bytes 49156
  0.7 17.1 %collective-permute-start.31 = (s32[8]{0:T(128)}, s32[8]{0:T(128)S(1)}, u32[]{:S(2)}, u32[]{:S(2)}) collective-permute-start(s32[8]{0:T(128)} %bitcast.39), channel_id=1, source_target_pairs={{0,480},{32,448},{64,416},{96,384},{128,352},{160,320},{192,288},{... | collective-permute-start | bytes 104 | tf_op jit(solution)/shard_map/ppermute | solution.py:23
  20.6 21.5 %copy-start.7 = (bf16[8,16,8192]{2,1,0:T(8,128)(2,1)S(1)}, bf16[8,16,8192]{2,1,0:T(8,128)(2,1)}, u32[]{:S(2)}) copy-start(bf16[8,16,8192]{2,1,0:T(8,128)(2,1)} %get-tuple-element.182.c) | copy-start | bytes 6291460 | tf_op jit(solution)/shard_map/cond
  20.6 57.2 %collective-permute-start.8 = (bf16[8,8192]{1,0:T(8,128)(2,1)S(1)}, bf16[8,8192]{1,0:T(8,128)(2,1)S(1)}, u32[]{:S(2)}, u32[]{:S(2)}) collective-permute-start(bf16[8,8192]{1,0:T(8,128)(2,1)S(1)} %get-tuple-element.184), channel_id=1, source_target_pairs={{0,480},{32,448},{64,416},{96,384},{128,352},{160,320},{192,288},{... | collective-permute-start | bytes 393224 | tf_op jit(solution)/shard_map/cond/branch_4_fun/ppermute | solution.py:23
  30.2 47.6 %collective-permute-start.9 = (bf16[1,8192]{1,0:T(2,128)(2,1)S(1)}, bf16[1,8192]{1,0:T(2,128)(2,1)S(1)}, u32[]{:S(2)}, u32[]{:S(2)}) collective-permute-start(bf16[1,8192]{1,0:T(2,128)(2,1)S(1)} %get-tuple-element.183.g), channel_id=1, source_target_pairs={{0,480},{32,448},{64,416},{96,384},{128,352},{160,320},{192,288},{... | collective-permute-start | bytes 49160 | tf_op jit(solution)/shard_map/cond/branch_4_fun/ppermute | solution.py:23
  32.7 58.0 %collective-permute-start.7 = (bf16[1,16,8192]{2,1,0:T(8,128)(2,1)S(1)}, bf16[1,16,8192]{2,1,0:T(8,128)(2,1)S(1)}, u32[]{:S(2)}, u32[]{:S(2)}) collective-permute-start(bf16[1,16,8192]{2,1,0:T(8,128)(2,1)S(1)} %branch_4_fun.4), channel_id=1, source_target_pairs={{0,480},{32,448},{64,416},{96,384},{128,352},{160,320},{192,288},{... | collective-permute-start | bytes 786440 | tf_op jit(solution)/shard_map/cond/branch_4_fun/ppermute | solution.py:23
  79.2 11.5 %collective-permute-start.10 = (f32[1,8320]{1,0:T(1,128)S(1)}, f32[1,8320]{1,0:T(1,128)S(1)}, u32[]{:S(2)}, u32[]{:S(2)}) collective-permute-start(f32[1,8320]{1,0:T(1,128)S(1)} %get-tuple-element.188), channel_id=1, source_target_pairs={{0,480},{32,448},{64,416},{96,384},{128,352},{160,320},{192,288},{... | collective-permute-start | bytes 99848 | tf_op jit(solution)/shard_map/cond/branch_4_fun/ppermute | solution.py:23
  92.8 29.2 %all-to-all-start = ((f32[32,1,256]{2,1,0:T(1,128)}), f32[32,1,256]{2,1,0:T(1,128)S(1)}, u32[]{:S(2)}, u32[]{:S(2)}) async-start(f32[32,1,256]{2,1,0:T(1,128)} %bitcast.4), calls=%async_computation | async-start | bytes 65536 | tf_op jit(solution)/shard_map/all_to_all | solution.py:297
  122.6 11.7 %all-to-all-start.1 = ((f32[32,1,256]{2,1,0:T(1,128)}), f32[32,1,256]{2,1,0:T(1,128)S(1)}, u32[]{:S(2)}, u32[]{:S(2)}) async-start(f32[32,1,256]{2,1,0:T(1,128)} %broadcast_in_dim.31), calls=%async_computation.1 | async-start | bytes 65536 | tf_op jit(solution)/shard_map/all_to_all | solution.py:299

commit v3 on v2

--- a/solution.py
+++ b/solution.py
@@ -292,12 +292,13 @@
     )(grad, back)
 
 
-def sum_over_dp(row):
-    size = lax.axis_size("dp")
-    shares = lax.all_to_all(row.reshape(size, -1), "dp", 0, 0)
+def share_over_dp(row):
+    return lax.all_to_all(row.reshape(lax.axis_size("dp"), -1), "dp", 0, 0)
+
+
+def whole_over_dp(shares):
     share = jnp.sum(shares, axis=0)
-    whole = lax.all_to_all(jnp.broadcast_to(share[None], (size,) + share.shape), "dp", 0, 0)
-    return whole.reshape(-1)
+    return lax.all_to_all(jnp.broadcast_to(share[None], shares.shape), "dp", 0, 0).reshape(-1)
 
 
 def shards(slab_store, slab_place, cotangent, norm_gain):
@@ -334,8 +335,8 @@
     row, inner, back = lax.switch(branch[0], branches[: 3 * MOST + 1], whole, half, cotangents)
 
     tokens = lax.axis_size("dp") * count * slab
-    gain_grad = sum_over_dp(row[0]) / math.sqrt(tokens)
-    places, row = lax.optimization_barrier((places, row))
+    shares, places = lax.optimization_barrier((share_over_dp(row[0]), places))
+    gain_grad = whole_over_dp(shares) / math.sqrt(tokens)
     away = (places >= slots).astype(jnp.int32)
     last = (away > 0) & (jnp.cumsum(away) == jnp.sum(away))
     inner_prods = jnp.sum(inner[:count], axis=-1) + jnp.where(last[:, None], back, 0.0)

time: 135 us -> 137 us (1.015); the launches traced: 135 us -> 135 us
  starting transfers between devices: 72.4 us -> 46 us
  waiting for transfers between devices: 46.8 us -> 70.1 us
  Pallas kernels: 9.81 us -> 11.9 us
    ppermute x5 -> x4, waiting for transfers between devices: 33.9 us -> 57 us  [mirror(): lax.ppermute(array, 'section', [(i, size - 1 - i) for i in range(size)])]
    all_to_all x2, starting transfers between devices: 25.4 us -> 8.27 us  [the longest x1 4.37 us: share_over_dp(): return lax.all_to_all(row.reshape(lax.axis_size('dp'), -1), 'dp', 0, 0)]
    ppermute x5 -> x4, starting transfers between devices: 47 us -> 37.8 us  [mirror(): lax.ppermute(array, 'section', [(i, size - 1 - i) for i in range(size)])]
    pallas_call x1, Pallas kernels: 4.15 us -> 6.58 us  [own_terms(): pl.pallas_call(functools.partial(own_kernel, slots), out_shape=(jax.Shape...]
  transfers between devices with their start and end apart: 7 -> 6, of which waited for: 5 -> 5; matrix products, arithmetic and copies ran while one was open for 2% -> 2% of each run, Pallas kernels for 5% -> 5%
where the time goes in v3:
time: 137 us; the launch traced here: 135 us
  waiting for transfers between devices  70.1 us (51%)
  starting transfers between devices  46 us (34%)
  Pallas kernels  11.9 us (9%)
  other arithmetic  3.13 us (2%)
  local copies, waits for them, and re-layouts  2.55 us (2%)
  between operations  1.38 us (1%)
    ppermute x4, waiting for transfers between devices, mirror(): lax.ppermute(array, 'section', [(i, size - 1 - i) for i in range(size)])  57 us
    ppermute x4, starting transfers between devices, mirror(): lax.ppermute(array, 'section', [(i, size - 1 - i) for i in range(size)])  37.8 us
    all_to_all x1, waiting for transfers between devices, share_over_dp(): return lax.all_to_all(row.reshape(lax.axis_size('dp'), -1), 'dp', 0, 0)  6.81 us
    pallas_call x1, Pallas kernels, own_terms(): pl.pallas_call(functools.partial(own_kernel, slots), out_shape=(jax.Shape...  6.58 us
    all_to_all x1, waiting for transfers between devices, whole_over_dp(): lax.all_to_all(jnp.broadcast_to(share[None], shares.shape), 'dp', 0, 0)  6.23 us
    all_to_all x1, starting transfers between devices, share_over_dp(): return lax.all_to_all(row.reshape(lax.axis_size('dp'), -1), 'dp', 0, 0)  4.37 us
    all_to_all x1, starting transfers between devices, whole_over_dp(): lax.all_to_all(jnp.broadcast_to(share[None], shares.shape), 'dp', 0, 0)  3.9 us
  transfers between devices with their start and end apart: 6, of which 5 were waited for; matrix products, arithmetic and copies ran while one was open for 2% of the time, Pallas kernels for 5%

profile of v3, /device:TPU:1, one launch (start us, length us, event | category | flops | bytes accessed | tf_op | source)
XLA Modules:
  0.0 135.1 jit_solution(225146317697658076)
XLA Ops:
  0.6 0.0 copy-start.17
  0.6 0.0 copy-start.3
  0.7 0.0 copy-start.16
  0.7 16.0 %collective-permute-start.31 = (s32[8]{0:T(128)}, s32[8]{0:T(128)S(1)}, u32[]{:S(2)}, u32[]{:S(2)}) collective-permute-start(s32[8]{0:T(128)} %bitcast.42), channel_id=1, source_target_pairs={{0,480},{32,448},{64,416},{96,384},{128,352},{160,320},{192,288},{... | collective-permute-start | bytes 104 | tf_op jit(solution)/shard_map/ppermute | solution.py:23
  16.7 1.0 collective-permute-done.31.far_places
  17.7 2.2 %shard_map.59 = (s32[1]{0:T(128)}, bf16[16,8192]{1,0:T(8,128)(2,1)S(1)}, bf16[8,8192]{1,0:T(8,128)(2,1)S(1)}) custom-call(s32[8]{0:T(128)} %bitcast.43, s32[8]{0:T(128)S(1)} %collective-permute-done.31.far_places, bf16[10,16,8192]{2,1,0:T(8,128)(2,1)} %bitcast.14, bf16[8,16,8192]{2,1,0:T(8,128)(2,1)} %bitcast.28), custom_call_target="tpu_custom_call" | custom-call | tf_op jit(solution)/shard_map/pallas_call | solution.py:90
  20.6 0.0 copy-done.17
  20.6 88.8 %conditional.1 = (f32[1,8192]{1,0:T(1,128)}, f32[9,16,128]{2,1,0:T(8,128)}, f32[1,16]{1,0:T(1,128)S(1)}) conditional(s32[]{:T(128)} %bitcast.3, (s32[8]{0:T(128)S(1)}, bf16[10,16,8192]{2,1,0:T(8,128)(2,1)S(1)}, bf16[8,16,8192]{2,1,0:T(8,128)(2,1)}, bf16[1,8192]{1,0:T(2,128)(2,1)S(1)}) %tuple.121, ...), branch_computations={%region_0.0_spmd, %region_1.0_spmd, %region_2.0_spmd, %region_3.0_... | conditional | flops 40000000000 | bytes 13257620 | solution.py:335
  20.6 0.0 copy-start.5
  20.6 9.5 %collective-permute-start.3 = (bf16[16,8192]{1,0:T(8,128)(2,1)S(1)}, bf16[16,8192]{1,0:T(8,128)(2,1)S(1)}, u32[]{:S(2)}, u32[]{:S(2)}) collective-permute-start(bf16[16,8192]{1,0:T(8,128)(2,1)S(1)} %get-tuple-element.161), channel_id=1, source_target_pairs={{0,480},{32,448},{64,416},{96,384},{128,352},{160,320},{192,288},{... | collective-permute-start | bytes 786440 | tf_op jit(solution)/shard_map/cond/branch_2_fun/ppermute | solution.py:23
  30.2 1.9 %collective-permute-start.4 = (bf16[1,8192]{1,0:T(2,128)(2,1)S(1)}, bf16[1,8192]{1,0:T(2,128)(2,1)S(1)}, u32[]{:S(2)}, u32[]{:S(2)}) collective-permute-start(bf16[1,8192]{1,0:T(2,128)(2,1)S(1)} %get-tuple-element.164.g), channel_id=1, source_target_pairs={{0,480},{32,448},{64,416},{96,384},{128,352},{160,320},{192,288},{... | collective-permute-start | bytes 49160 | tf_op jit(solution)/shard_map/cond/branch_2_fun/ppermute | solution.py:23
  32.1 6.6 %branch_2_fun.3 = (f32[8,8192]{1,0:T(8,128)S(1)}, f32[9,16,128]{2,1,0:T(8,128)}) custom-call(s32[8]{0:T(128)S(1)} %get-tuple-element.159.places, bf16[10,16,8192]{2,1,0:T(8,128)(2,1)S(1)} %get-tuple-element.162.x, bf16[8,16,8192]{2,1,0:T(8,128)(2,1)} %get-tuple-element.163.c, bf16[1,8192]{1,0:T(2,128)(2,1)S(1)} %get-tuple-element.164.g), custom_call_target="tpu_custom_call" | custom-call | tf_op jit(solution)/shard_map/cond/branch_2_fun/pallas_call | solution.py:213
  38.7 54.7 %collective-permute-done.4.far_g = bf16[1,8192]{1,0:T(2,128)(2,1)S(1)} collective-permute-done((bf16[1,8192]{1,0:T(2,128)(2,1)S(1)}, bf16[1,8192]{1,0:T(2,128)(2,1)S(1)}, u32[]{:S(2)}, u32[]{:S(2)}) %collective-permute-start.4) | collective-permute-done | bytes 16416 | tf_op jit(solution)/shard_map/cond/branch_2_fun/ppermute | solution.py:23
  93.4 0.0 collective-permute-done.3.y
  93.4 1.5 %branch_2_fun.4 = (f32[8,8192]{1,0:T(8,128)S(1)}, f32[9,16,128]{2,1,0:T(8,128)}, f32[1,8320]{1,0:T(1,128)S(1)}) custom-call(s32[8]{0:T(128)S(1)} %get-tuple-element.159.places, s32[8]{0:T(128)S(1)} %get-tuple-element.160.far_places, bf16[16,8192]{1,0:T(8,128)(2,1)S(1)} %collective-permute-done.3.y, ...), custom_call_target="tpu_custom_call", output_to_operand_aliasing={{1}: (8, {})} | custom-call | flops 40000000000 | bytes 1000000 | tf_op jit(solution)/shard_map/cond/branch_2_fun/pallas_call | solution.py:164
  94.8 0.7 copy-done.1
  95.5 10.3 %collective-permute-start.5 = (f32[1,8320]{1,0:T(1,128)S(1)}, f32[1,8320]{1,0:T(1,128)S(1)}, u32[]{:S(2)}, u32[]{:S(2)}) collective-permute-start(f32[1,8320]{1,0:T(1,128)S(1)} %get-tuple-element.168), channel_id=1, source_target_pairs={{0,480},{32,448},{64,416},{96,384},{128,352},{160,320},{192,288},{... | collective-permute-start | bytes 99848 | tf_op jit(solution)/shard_map/cond/branch_2_fun/ppermute | solution.py:23
  105.9 1.3 collective-permute-done.5.back
  107.2 0.6 copy-done.19
  107.8 1.6 %branch_2_fun.5 = f32[1,8192]{1,0:T(1,128)} custom-call(f32[8,8192]{1,0:T(8,128)} %copy-done.1, f32[1,8320]{1,0:T(1,128)} %copy-done.19), custom_call_target="tpu_custom_call" | custom-call | tf_op jit(solution)/shard_map/cond/branch_2_fun/pallas_call | solution.py:287
  109.4 4.4 %all-to-all-start = ((f32[32,1,256]{2,1,0:T(1,128)}), f32[32,1,256]{2,1,0:T(1,128)S(1)}, u32[]{:S(2)}, u32[]{:S(2)}) async-start(f32[32,1,256]{2,1,0:T(1,128)} %bitcast.4), calls=%async_computation | async-start | bytes 65536 | tf_op jit(solution)/shard_map/all_to_all | solution.py:296
  113.8 0.9 slice_reduce_fusion
  114.7 6.8 %all-to-all-done = f32[32,1,256]{2,1,0:T(1,128)S(1)} async-done(((f32[32,1,256]{2,1,0:T(1,128)}), f32[32,1,256]{2,1,0:T(1,128)S(1)}, u32[]{:S(2)}, u32[]{:S(2)}) %all-to-all-start) | async-done | bytes 32800 | tf_op jit(solution)/shard_map/all_to_all | solution.py:296
  121.6 0.6 fusion
  122.2 0.6 broadcast_in_dim.31
  122.8 3.9 %all-to-all-start.1 = ((f32[32,1,256]{2,1,0:T(1,128)}), f32[32,1,256]{2,1,0:T(1,128)S(1)}, u32[]{:S(2)}, u32[]{:S(2)}) async-start(f32[32,1,256]{2,1,0:T(1,128)} %broadcast_in_dim.31), calls=%async_computation.1 | async-start | bytes 65536 | tf_op jit(solution)/shard_map/all_to_all | solution.py:301
  126.7 0.2 reduce-window.9
  126.9 0.7 bitcast_and_fusion
  127.6 0.1 add_multiply_fusion
  127.7 0.6 div.21
  128.3 6.2 %all-to-all-done.1 = f32[32,1,256]{2,1,0:T(1,128)S(1)} async-done(((f32[32,1,256]{2,1,0:T(1,128)}), f32[32,1,256]{2,1,0:T(1,128)S(1)}, u32[]{:S(2)}, u32[]{:S(2)}) %all-to-all-start.1) | async-done | bytes 32800 | tf_op jit(solution)/shard_map/all_to_all | solution.py:301
  134.5 0.6 broadcast_multiply_fusion
  (9 shorter events, 0.0 us)
Async XLA Ops:
  0.6 19.9 %copy-start.17 = (s32[1,1,8]{2,1,0:T(1,128)S(1)}, s32[1,1,8]{2,1,0:T(1,128)}, u32[]{:S(2)}) copy-start(s32[1,1,8]{2,1,0:T(1,128)} %param.18) | copy-start | bytes 100
  0.6 19.9 %copy-start.3 = (bf16[1,1,10,16,8192]{4,3,2,1,0:T(8,128)(2,1)S(1)}, bf16[1,1,10,16,8192]{4,3,2,1,0:T(8,128)(2,1)}, u32[]{:S(2)}) copy-start(bf16[1,1,10,16,8192]{4,3,2,1,0:T(8,128)(2,1)} %param.17) | copy-start | bytes 7864324
  0.7 19.9 %copy-start.16 = (bf16[1,8192]{1,0:T(2,128)(2,1)S(1)}, bf16[1,8192]{1,0:T(2,128)(2,1)}, u32[]{:S(2)}) copy-start(bf16[1,8192]{1,0:T(2,128)(2,1)} %param.20) | copy-start | bytes 49156
  0.7 17.1 %collective-permute-start.31 = (s32[8]{0:T(128)}, s32[8]{0:T(128)S(1)}, u32[]{:S(2)}, u32[]{:S(2)}) collective-permute-start(s32[8]{0:T(128)} %bitcast.42), channel_id=1, source_target_pairs={{0,480},{32,448},{64,416},{96,384},{128,352},{160,320},{192,288},{... | collective-permute-start | bytes 104 | tf_op jit(solution)/shard_map/ppermute | solution.py:23
  20.6 72.7 %copy-start.5 = (bf16[8,16,8192]{2,1,0:T(8,128)(2,1)S(1)}, bf16[8,16,8192]{2,1,0:T(8,128)(2,1)}, u32[]{:S(2)}) copy-start(bf16[8,16,8192]{2,1,0:T(8,128)(2,1)} %get-tuple-element.163.c) | copy-start | bytes 6291460 | tf_op jit(solution)/shard_map/cond
  20.6 72.7 %collective-permute-start.3 = (bf16[16,8192]{1,0:T(8,128)(2,1)S(1)}, bf16[16,8192]{1,0:T(8,128)(2,1)S(1)}, u32[]{:S(2)}, u32[]{:S(2)}) collective-permute-start(bf16[16,8192]{1,0:T(8,128)(2,1)S(1)} %get-tuple-element.161), channel_id=1, source_target_pairs={{0,480},{32,448},{64,416},{96,384},{128,352},{160,320},{192,288},{... | collective-permute-start | bytes 786440 | tf_op jit(solution)/shard_map/cond/branch_2_fun/ppermute | solution.py:23
  30.2 63.2 %collective-permute-start.4 = (bf16[1,8192]{1,0:T(2,128)(2,1)S(1)}, bf16[1,8192]{1,0:T(2,128)(2,1)S(1)}, u32[]{:S(2)}, u32[]{:S(2)}) collective-permute-start(bf16[1,8192]{1,0:T(2,128)(2,1)S(1)} %get-tuple-element.164.g), channel_id=1, source_target_pairs={{0,480},{32,448},{64,416},{96,384},{128,352},{160,320},{192,288},{... | collective-permute-start | bytes 49160 | tf_op jit(solution)/shard_map/cond/branch_2_fun/ppermute | solution.py:23
  94.8 0.7 copy-start.1
  95.5 11.6 %collective-permute-start.5 = (f32[1,8320]{1,0:T(1,128)S(1)}, f32[1,8320]{1,0:T(1,128)S(1)}, u32[]{:S(2)}, u32[]{:S(2)}) collective-permute-start(f32[1,8320]{1,0:T(1,128)S(1)} %get-tuple-element.168), channel_id=1, source_target_pairs={{0,480},{32,448},{64,416},{96,384},{128,352},{160,320},{192,288},{... | collective-permute-start | bytes 99848 | tf_op jit(solution)/shard_map/cond/branch_2_fun/ppermute | solution.py:23
  107.2 0.6 copy-start.19
  109.4 12.1 %all-to-all-start = ((f32[32,1,256]{2,1,0:T(1,128)}), f32[32,1,256]{2,1,0:T(1,128)S(1)}, u32[]{:S(2)}, u32[]{:S(2)}) async-start(f32[32,1,256]{2,1,0:T(1,128)} %bitcast.4), calls=%async_computation | async-start | bytes 65536 | tf_op jit(solution)/shard_map/all_to_all | solution.py:296
  122.8 11.6 %all-to-all-start.1 = ((f32[32,1,256]{2,1,0:T(1,128)}), f32[32,1,256]{2,1,0:T(1,128)S(1)}, u32[]{:S(2)}, u32[]{:S(2)}) async-start(f32[32,1,256]{2,1,0:T(1,128)} %broadcast_in_dim.31), calls=%async_computation.1 | async-start | bytes 65536 | tf_op jit(solution)/shard_map/all_to_all | solution.py:301
